TPU v7x, 128 devices: a whole 4x4x4 slice. The times are simulated.
128 devices in a mesh: row: 16 (over y, x), col: 8 (over z, core).
Axes of the slice: x: 4, y: 4, z: 4, core: 2. Of those that a mesh axis runs over, the one named last changes fastest.
Arguments:
- upper_block: float32 [2, 1024, 1024], P(None, 'row', 'col'), may hold values from -0.25 to 0.25
- block_inverse: float32 [2, 1024, 64], P(None, 'row'), may hold values from -0.375 to 0.375
- panel_rhs: float32 [2, 32, 1024], P(None, None, 'row'), may hold values from -6 to 6
- upper_trail: float32 [2, 1024, 131072], P(None, 'row', 'col'), may hold values from -0.125 to 0.125
- trail_rhs: float32 [2, 32, 131072], P(None, None, ('col', 'row')), may hold values from -6 to 6
- currents: float32 [2, 1024], P(None, 'row'), may hold values from -4 to 4
- owner: int32 [1024], P('row'), may hold values from 0 to 511
Outputs:
- panel_adjoint: float32 [2, 32, 1024], P(None, None, 'row')
- trail_updated: float32 [2, 32, 131072], P(None, None, ('col', 'row'))
- patch_gradient: float32 [512], P(('row', 'col'))
Inputs may be any that keep to these rules, and one draw needn't show every extreme that they name: owner names a surface patch for each panel unknown.
All inputs are finite; a program needn't handle non-finite values.
Results may differ from a plain program's by a relative error of at most 0.0003.
Values sent between devices are 32-bit elements; how exact they have to be, the bound alone decides.
A program may use at most 64 MiB of HBM per device.

v0:
```python
import jax
import jax.numpy as jnp
from jax import lax
from jax.sharding import Mesh
from jax.sharding import PartitionSpec as P

PATCH_DEV = 4
ROW = ("row_0", "row_1")
ROW_COL = ("row_0", "row_1", "col")
COL_ROW = ("col", "row_0", "row_1")
highest = lax.Precision.HIGHEST


def rows_first(arrays, axis, dims):
    turned = [jnp.moveaxis(a, dim, 0) for a, dim in zip(arrays, dims)]
    widths = [t[0].size for t in turned]
    both = jnp.concatenate([t.reshape(-1, w) for t, w in zip(turned, widths)], axis=1)
    filled = lax.all_gather(both, axis, axis=0, tiled=True)
    pieces = jnp.split(filled, [sum(widths[:k]) for k in range(1, len(widths))], axis=1)
    return tuple(
        (
            jnp.moveaxis(b.reshape(-1, *t.shape[1:]), 0, dim)
            for b, t, dim in zip(pieces, turned, dims)
        )
    )


def sum_by_axis(value, axes, dim):
    if not axes:
        return value
    nearer = lax.psum_scatter(value, axes[0], scatter_dimension=dim, tiled=True)
    return sum_by_axis(nearer, axes[1:], dim)


def product_high(first, second):
    return jnp.dot(first, second, precision=highest, preferred_element_type=jnp.float32)


def conj_product(left, right):
    real_part = product_high(left[0], right[0]) + product_high(left[1], right[1])
    imag_part = product_high(left[1], right[0]) - product_high(left[0], right[1])
    return jnp.stack([real_part, imag_part])


def sweep(upper, inverses, rhs, width):
    count = rhs.shape[2] // width
    held_start = jnp.zeros(rhs.shape, jnp.float32)
    solved_start = jnp.zeros(rhs.shape, jnp.float32)

    def advance(index, carry):
        held, solved = carry
        start = (jnp.asarray(index) * width).astype(jnp.int32)
        local = lax.dynamic_slice_in_dim(held, start, width, 2)
        residual = lax.dynamic_slice_in_dim(rhs, start, width, 2) - local
        inverse = lax.dynamic_slice_in_dim(inverses, start, width, 1)
        value = conj_product(residual, inverse)
        rows_here = lax.dynamic_slice_in_dim(upper, start, width, 1)
        held = held + conj_product(value, rows_here)
        solved = lax.dynamic_update_slice_in_dim(solved, value, start, 2)
        return (held, solved)

    return lax.fori_loop(0, count, advance, (held_start, solved_start))[1]


def on_device(upper_block, block_inverse, panel_rhs, upper_trail, trail_rhs, currents, owner):
    rows_count = lax.axis_size(ROW)
    cols_count = lax.axis_size("col")
    row_index = lax.axis_index(ROW)
    col_index = lax.axis_index("col")
    width = block_inverse.shape[1]
    whole_rows, inverses, rhs_all = rows_first(
        (upper_block, block_inverse, panel_rhs), ROW, (1, 1, 2)
    )
    whole = lax.all_gather(whole_rows, "col", axis=2, tiled=True)
    solved_all = sweep(whole, inverses, rhs_all, width)
    solved = lax.dynamic_slice_in_dim(solved_all, row_index * width, width, 2)
    term = conj_product(solved, upper_trail)
    reduced = sum_by_axis(term, ROW, 2)
    updated = trail_rhs - reduced
    share = width // cols_count
    start = col_index * share
    mine = lax.dynamic_slice_in_dim(solved, start, share, 2)
    total = jnp.sum(mine, axis=1)
    current_part = lax.dynamic_slice_in_dim(currents, start, share, 1)
    owner_part = lax.dynamic_slice_in_dim(owner, start, share, 0)
    partial_value = current_part[0] * total[0] - current_part[1] * total[1]
    patch_count = PATCH_DEV * rows_count * cols_count
    patch_ids = lax.broadcasted_iota(jnp.int32, (share, patch_count), 1)
    selector = (owner_part[:, None] == patch_ids).astype(jnp.float32)
    spread = product_high(partial_value[None, :], selector)[0]
    gradient = lax.psum_scatter(spread, ROW_COL, scatter_dimension=0, tiled=True)
    return (solved, updated, gradient)


def solution(mesh):
    split = Mesh(mesh.devices.reshape(4, 4, mesh.shape["col"]), ("row_0", "row_1", "col"))
    return jax.shard_map(
        on_device,
        mesh=split,
        in_specs=(
            P(None, ROW, "col"),
            P(None, ROW, None),
            P(None, None, ROW),
            P(None, ROW, "col"),
            P(None, None, COL_ROW),
            P(None, ROW),
            P(ROW),
        ),
        out_specs=(P(None, None, ROW), P(None, None, COL_ROW), P(ROW_COL)),
        check_vma=False,
    )
```

profile of v0, /device:TPU:1, one launch (start us, length us, event | category | flops | bytes accessed | tf_op | source)
XLA Modules:
  0.0 364.6 jit_solution(3339413474390331940)
XLA Ops:
  9.8 48.1 %all-gather.3.cloned.1.call-done = f32[1024,448]{1,0:T(8,128)} async-done(((f32[64,448]{1,0:T(8,128)}), f32[1024,448]{1,0:T(8,128)}) %all-gather.3.cloned.1.call-update) | async-done | bytes 1835024 | tf_op jit(solution)/shard_map/all_gather | solution.py:18
  57.9 1.4 split.14
  59.3 1.3 copy.31
  61.2 50.3 %all-gather.5.cloned.1.call-done = f32[2,1024,1024]{1,2,0:T(8,128)} async-done(((f32[2,1024,128]{1,2,0:T(8,128)}), f32[2,1024,1024]{1,2,0:T(8,128)}) %all-gather.5.cloned.1.call-update) | async-done | bytes 8388624 | tf_op jit(solution)/shard_map/all_gather | solution.py:74
  111.4 8.7 %copy.33 = f32[2,1024,1024]{2,1,0:T(8,128)} copy(f32[2,1024,1024]{1,2,0:T(8,128)} %all-gather.5.cloned.1.call-done) | data formatting | bytes 16777216
  120.1 106.3 %while.16 = (s32[]{:T(128)}, f32[2,32,1024]{2,1,0:T(8,128)S(1)}, f32[2,32,1024]{2,1,0:T(8,128)S(1)}, f32[2,32,1024]{2,1,0:T(8,128)S(1)}, f32[2,1024,64]{1,2,0:T(...) while((s32[]{:T(128)}, f32[2,32,1024]{2,1,0:T(8,128)S(1)}, ...), condition=%wide.region_1.0_spmd.clone, body=%wide.region_0.0_spmd.clone.sunk | while | flops 107294728 | bytes 3555570 | solution.py:62
  120.8 1.2 fusion.58
  122.5 1.2 fusion.60
  127.3 1.2 fusion.58
  129.0 1.2 fusion.60
  131.4 1.2 fusion.62
  134.1 1.2 fusion.58
  135.8 1.2 fusion.60
  138.2 1.2 fusion.62
  140.6 1.2 fusion.58
  142.3 1.2 fusion.60
  147.4 1.2 fusion.58
  149.1 1.2 fusion.60
  151.6 1.2 fusion.62
  155.6 1.2 fusion.60
  158.1 1.2 fusion.62
  160.7 1.2 fusion.58
  162.4 1.2 fusion.60
  164.9 1.2 fusion.62
  167.2 1.2 fusion.58
  168.9 1.2 fusion.60
  175.7 1.2 fusion.60
  178.2 1.2 fusion.62
  182.2 1.2 fusion.60
  187.3 1.2 fusion.58
  189.0 1.2 fusion.60
  195.5 1.2 fusion.60
  198.0 1.2 fusion.62
  202.3 1.2 fusion.60
  207.1 1.2 fusion.58
  208.8 1.2 fusion.60
  215.6 1.2 fusion.60
  218.1 1.2 fusion.62
  222.1 1.2 fusion.60
  224.5 1.2 fusion.62
  226.4 4.0 %fusion.20 = f32[32,16384]{1,0:T(8,128)S(1)} fusion(f32[2,64,16384]{2,1,0:T(8,128)} %param.12, f32[2,32,1024]{2,1,0:T(8,128)S(1)} %get-tuple-element.112, s32[]{:T(128)S(6)} %select_n.23), kind=kOutput, calls=%fused_computation.37 | convolution fusion | flops 402653184 | bytes 6307844 | tf_op jit(solution)/shard_map/dot_general | solution.py:36
  230.5 4.0 %fusion.18 = f32[32,16384]{1,0:T(8,128)S(1)} fusion(f32[2,64,16384]{2,1,0:T(8,128)} %param.12, f32[2,32,1024]{2,1,0:T(8,128)S(1)} %get-tuple-element.112, s32[]{:T(128)S(6)} %add.84, s32[]{:T(128)S(6)} %select_n.23), kind=kOutput, calls=%fused_computation.35 | convolution fusion | flops 402653184 | bytes 6307848 | tf_op jit(solution)/shard_map/dot_general | solution.py:36
  234.5 3.9 %fusion.14 = f32[1,32,16384]{2,1,0:T(8,128)S(1)} fusion(f32[32,16384]{1,0:T(8,128)S(1)} %fusion.18, f32[2,64,16384]{2,1,0:T(8,128)} %param.12, f32[2,32,1024]{2,1,0:T(8,128)S(1)} %get-tuple-element.112, s32[]{:T(128)S(6)} %select_n.23), kind=kOutput, calls=%fused_computation.29 | convolution fusion | flops 403177472 | bytes 8404996 | tf_op jit(solution)/shard_map/dot_general | solution.py:36
  238.5 2.2 fusion.15
  240.7 2.2 pad_maximum_fusion.1
  243.0 46.6 %reduce-scatter.3.cloned.1.call-done = f32[2,32,4096]{2,1,0:T(8,128)} async-done(((f32[2,32,16384]{2,1,0:T(8,128)}), f32[2,32,4096]{2,1,0:T(8,128)}) %reduce-scatter.3.cloned.1.call-update) | async-done | bytes 1048592 | tf_op jit(solution)/shard_map/reduce_scatter | solution.py:31
  290.1 65.0 %all-reduce = f32[512]{0:T(512)S(1)} all-reduce(f32[512]{0:T(512)S(1)} %bitcast.133), channel_id=4, replica_groups=mesh['row_0'=4,'row_1'=4,'col'=8] {'row_0','row_1','col'}, use_global_device_ids=true, to_apply=%region_5.0.clone | all-reduce | flops 512 | bytes 4096
  356.4 1.7 sub.32
  (215 shorter events, 67.6 us)
Async XLA Ops:
  7.2 1.9 copy-start
  7.2 50.8 %all-gather.3.cloned.1.call-start = ((), (), s32[]{:S(2)}) async-start(), calls=%async_computation.2 | async-start | bytes 2228224 | tf_op jit(solution)/shard_map/all_gather | solution.py:18
  9.8 101.7 %all-gather.5.cloned.1.call-start = ((), (), s32[]{:S(2)}) async-start(), calls=%async_computation.3 | async-start | bytes 9437184 | tf_op jit(solution)/shard_map/all_gather | solution.py:74
  57.9 2.8 slice-start.2
  57.9 3.0 slice-start.3
  60.7 228.9 %reduce-scatter.3.cloned.1.call-start = ((), (), s32[]{:S(2)}) async-start(), calls=%async_computation.4 | async-start | bytes 5242880 | tf_op jit(solution)/shard_map/reduce_scatter | solution.py:31
  226.4 12.1 %slice-start = ((s8[8388608]{0:T(1024)(128)(4,1)}), s8[4194304]{0:T(1024)(128)(4,1)S(1)}, s32[]{:S(2)}) async-start(s8[8388608]{0:T(1024)(128)(4,1)} %bitcast.124), calls=%async_computation.6 | async-start | bytes 8388608
  230.5 8.0 %slice-start.1 = ((s8[8388608]{0:T(1024)(128)(4,1)}), s8[4194304]{0:T(1024)(128)(4,1)S(1)}, s32[]{:S(2)}) async-start(s8[8388608]{0:T(1024)(128)(4,1)} %bitcast.124), calls=%async_computation.7 | async-start | bytes 8388608
  242.9 46.7 %copy-start.3 = (s32[64]{0:T(128)S(1)}, s32[64]{0:T(128)}, u32[]{:S(2)}) copy-start(s32[64]{0:T(128)} %param.15) | copy-start | bytes 772
  242.9 46.8 %copy-start.2 = (f32[2,64]{1,0:T(2,128)S(1)}, f32[2,64]{1,0:T(2,128)}, u32[]{:S(2)}) copy-start(f32[2,64]{1,0:T(2,128)} %param.14) | copy-start | bytes 1540
  242.9 113.4 %copy-start.1 = (f32[2,32,1024]{2,1,0:T(8,128)S(1)}, f32[2,32,1024]{2,1,0:T(8,128)}, u32[]{:S(2)}) copy-start(f32[2,32,1024]{2,1,0:T(8,128)} %param.13) | copy-start | bytes 786436
  243.0 113.4 %reduce-scatter.5.cloned.1.call-start = ((), (), s32[]{:S(2)}) async-start(), calls=%async_computation.5 | async-start | bytes 1310720 | tf_op jit(solution)/shard_map/reduce_scatter | solution.py:31
Sparse Core Ops, SparseCore 0:
  10.7 47.1 all-gather.2
  60.8 50.5 all-gather.4
  243.1 46.4 reduce-scatter.2
  292.0 20.9 reduce-scatter.4
where the time goes:
time: 367 us; the launch traced here: 365 us
  waiting for transfers between devices  145 us (40%)
  matrix products  108 us (29%)
  blocking collectives  65 us (18%)
  local copies, waits for them, and re-layouts  22.7 us (6%)
  between operations  13.9 us (4%)
  other arithmetic  7.86 us (2%)
    dot_general x133, matrix products, product_high(): jnp.dot(first, second, precision=highest, preferred_element_type=jnp.floa...  108 us
    unnamed x1, blocking collectives  65 us
    all_gather x1, waiting for transfers between devices, on_device(): whole = lax.all_gather(whole_rows, 'col', axis=2, tiled=True)  50.3 us
    all_gather x1, waiting for transfers between devices, rows_first(): filled = lax.all_gather(both, axis, axis=0, tiled=True)  48.1 us
    reduce_scatter x2, waiting for transfers between devices, sum_by_axis(): nearer = lax.psum_scatter(value, axes[0], scatter_dimension=dim, tiled=True)  46.6 us
    unnamed x14, local copies, waits for them, and re-layouts  9.29 us
    dynamic_update_slice x16, local copies, waits for them, and re-layouts, advance(): solved = lax.dynamic_update_slice_in_dim(solved, value, start, 2)  7.65 us
  transfers between devices with their start and end apart: 4, of which 3 were waited for; matrix products, arithmetic and copies ran while one was open for 1% of the time, Pallas kernels for 0%

commit v1 on v0

--- a/solution.py
+++ b/solution.py
@@ -15,7 +15,12 @@
     turned = [jnp.moveaxis(a, dim, 0) for a, dim in zip(arrays, dims)]
     widths = [t[0].size for t in turned]
     both = jnp.concatenate([t.reshape(-1, w) for t, w in zip(turned, widths)], axis=1)
-    filled = lax.all_gather(both, axis, axis=0, tiled=True)
+    filled = jnp.concatenate(
+        jax.lax.all_to_all(
+            jnp.stack([both] * jax.lax.axis_size(axis)), axis_name=axis, split_axis=0, concat_axis=0
+        ),
+        axis=0,
+    )
     pieces = jnp.split(filled, [sum(widths[:k]) for k in range(1, len(widths))], axis=1)
     return tuple(
         (

time: 367 us -> 351 us (0.956)
  waiting for transfers between devices: 145 us -> 96.3 us
  blocking collectives: 65 us -> 99.7 us
    all_gather x1 -> x0, waiting for transfers between devices: 48.1 us -> none  [rows_first(): filled = lax.all_gather(both, axis, axis=0, tiled=True)]
    all_to_all x0 -> x1, blocking collectives: none -> 34.7 us  [rows_first(): jax.lax.all_to_all(jnp.stack([both] * jax.lax.axis_size(axis)), axis_name...]
  transfers between devices with their start and end apart: 4 -> 3, of which waited for: 3 -> 2; matrix products, arithmetic and copies ran while one was open for 1% -> 1% of each run, Pallas kernels for 0% -> 0%
where the time goes in v1:
time: 351 us; the launch traced here: 349 us
  matrix products  108 us (31%)
  blocking collectives  99.7 us (28%)
  waiting for transfers between devices  96.3 us (27%)
  local copies, waits for them, and re-layouts  21.9 us (6%)
  between operations  13.9 us (4%)
  other arithmetic  7.2 us (2%)
    dot_general x133, matrix products, product_high(): jnp.dot(first, second, precision=highest, preferred_element_type=jnp.floa...  108 us
    unnamed x1, blocking collectives  64.9 us
    all_gather x1, waiting for transfers between devices, on_device(): whole = lax.all_gather(whole_rows, 'col', axis=2, tiled=True)  49.7 us
    reduce_scatter x2, waiting for transfers between devices, sum_by_axis(): nearer = lax.psum_scatter(value, axes[0], scatter_dimension=dim, tiled=True)  46.6 us
    all_to_all x1, blocking collectives, rows_first(): jax.lax.all_to_all(jnp.stack([both] * jax.lax.axis_size(axis)), axis_name...  34.7 us
    unnamed x14, local copies, waits for them, and re-layouts  9.3 us
    dynamic_update_slice x16, local copies, waits for them, and re-layouts, advance(): solved = lax.dynamic_update_slice_in_dim(solved, value, start, 2)  7.65 us
  transfers between devices with their start and end apart: 3, of which 2 were waited for; matrix products, arithmetic and copies ran while one was open for 1% of the time, Pallas kernels for 0%

profile of v1, /device:TPU:1, one launch (start us, length us, event | category | flops | bytes accessed | tf_op | source)
XLA Modules:
  0.0 349.0 jit_solution(11621978427025995279)
XLA Ops:
  9.4 34.7 %all_to_all.5 = f32[16,64,448]{2,1,0:T(8,128)S(1)} all-to-all(f32[16,64,448]{2,1,0:T(8,128)S(1)} %stack.70), channel_id=1, replica_groups=mesh['row_0'=4,'row_1'=4,'col'=8] {'row_0','row_1'}, dimensions={0} | all-to-all | bytes 3670016 | tf_op jit(solution)/shard_map/all_to_all | solution.py:19
  44.2 1.4 copy.31
  46.2 49.7 %all-gather.2.cloned.1.call-done = f32[2,1024,1024]{1,2,0:T(8,128)} async-done(((f32[2,1024,128]{1,2,0:T(8,128)}), f32[2,1024,1024]{1,2,0:T(8,128)}) %all-gather.2.cloned.1.call-update) | async-done | bytes 8388624 | tf_op jit(solution)/shard_map/all_gather | solution.py:79
  95.9 8.7 %copy.33 = f32[2,1024,1024]{2,1,0:T(8,128)} copy(f32[2,1024,1024]{1,2,0:T(8,128)} %all-gather.2.cloned.1.call-done) | data formatting | bytes 16777216
  104.6 106.3 %while.16 = (s32[]{:T(128)}, f32[2,32,1024]{2,1,0:T(8,128)S(1)}, f32[2,32,1024]{2,1,0:T(8,128)S(1)}, f32[2,32,1024]{2,1,0:T(8,128)S(1)}, f32[2,1024,64]{1,2,0:T(...) while((s32[]{:T(128)}, f32[2,32,1024]{2,1,0:T(8,128)S(1)}, ...), condition=%wide.region_1.0_spmd.clone, body=%wide.region_0.0_spmd.clone.sunk | while | flops 107294728 | bytes 3555570 | solution.py:67
  105.3 1.2 fusion.58
  107.0 1.2 fusion.60
  109.5 1.2 fusion.62
  111.8 1.2 fusion.58
  113.5 1.2 fusion.60
  118.6 1.2 fusion.58
  120.3 1.2 fusion.60
  122.8 1.2 fusion.62
  126.8 1.2 fusion.60
  129.3 1.2 fusion.62
  131.9 1.2 fusion.58
  133.6 1.2 fusion.60
  136.1 1.2 fusion.62
  138.4 1.2 fusion.58
  140.1 1.2 fusion.60
  142.6 1.2 fusion.62
  145.2 1.2 fusion.58
  146.9 1.2 fusion.60
  149.4 1.2 fusion.62
  151.7 1.2 fusion.58
  153.4 1.2 fusion.60
  158.5 1.2 fusion.58
  160.2 1.2 fusion.60
  162.7 1.2 fusion.62
  166.8 1.2 fusion.60
  169.2 1.2 fusion.62
  173.5 1.2 fusion.60
  178.3 1.2 fusion.58
  180.1 1.2 fusion.60
  186.8 1.2 fusion.60
  189.3 1.2 fusion.62
  193.4 1.2 fusion.60
  198.4 1.2 fusion.58
  200.2 1.2 fusion.60
  206.6 1.2 fusion.60
  210.9 4.0 %fusion.20 = f32[32,16384]{1,0:T(8,128)S(1)} fusion(f32[2,64,16384]{2,1,0:T(8,128)} %param.12, f32[2,32,1024]{2,1,0:T(8,128)S(1)} %get-tuple-element.112, s32[]{:T(128)S(6)} %select_n.23), kind=kOutput, calls=%fused_computation.37 | convolution fusion | flops 402653184 | bytes 6307844 | tf_op jit(solution)/shard_map/dot_general | solution.py:41
  215.0 4.1 %fusion.18 = f32[32,16384]{1,0:T(8,128)S(1)} fusion(f32[2,64,16384]{2,1,0:T(8,128)} %param.12, f32[2,32,1024]{2,1,0:T(8,128)S(1)} %get-tuple-element.112, s32[]{:T(128)S(6)} %add.84, s32[]{:T(128)S(6)} %select_n.23), kind=kOutput, calls=%fused_computation.35 | convolution fusion | flops 402653184 | bytes 6307848 | tf_op jit(solution)/shard_map/dot_general | solution.py:41
  219.1 3.9 %fusion.14 = f32[1,32,16384]{2,1,0:T(8,128)S(1)} fusion(f32[32,16384]{1,0:T(8,128)S(1)} %fusion.18, f32[2,64,16384]{2,1,0:T(8,128)} %param.12, f32[2,32,1024]{2,1,0:T(8,128)S(1)} %get-tuple-element.112, s32[]{:T(128)S(6)} %select_n.23), kind=kOutput, calls=%fused_computation.29 | convolution fusion | flops 403177472 | bytes 8404996 | tf_op jit(solution)/shard_map/dot_general | solution.py:41
  223.0 2.2 fusion.15
  225.2 2.2 pad_maximum_fusion.1
  227.5 46.6 %reduce-scatter.3.cloned.1.call-done = f32[2,32,4096]{2,1,0:T(8,128)} async-done(((f32[2,32,16384]{2,1,0:T(8,128)}), f32[2,32,4096]{2,1,0:T(8,128)}) %reduce-scatter.3.cloned.1.call-update) | async-done | bytes 1048592 | tf_op jit(solution)/shard_map/reduce_scatter | solution.py:36
  274.6 64.9 %all-reduce = f32[512]{0:T(512)S(1)} all-reduce(f32[512]{0:T(512)S(1)} %bitcast.137), channel_id=4, replica_groups=mesh['row_0'=4,'row_1'=4,'col'=8] {'row_0','row_1','col'}, use_global_device_ids=true, to_apply=%region_5.0.clone | all-reduce | flops 512 | bytes 4096
  340.8 1.7 sub.32
  (212 shorter events, 66.2 us)
Async XLA Ops:
  7.2 1.9 copy-start
  7.2 88.8 %all-gather.2.cloned.1.call-start = ((), (), s32[]{:S(2)}) async-start(), calls=%async_computation.3 | async-start | bytes 9437184 | tf_op jit(solution)/shard_map/all_gather | solution.py:79
  45.6 228.5 %reduce-scatter.3.cloned.1.call-start = ((), (), s32[]{:S(2)}) async-start(), calls=%async_computation.4 | async-start | bytes 5242880 | tf_op jit(solution)/shard_map/reduce_scatter | solution.py:36
  210.9 12.1 %slice-start = ((s8[8388608]{0:T(1024)(128)(4,1)}), s8[4194304]{0:T(1024)(128)(4,1)S(1)}, s32[]{:S(2)}) async-start(s8[8388608]{0:T(1024)(128)(4,1)} %bitcast.125), calls=%async_computation.6 | async-start | bytes 8388608
  215.0 8.0 %slice-start.1 = ((s8[8388608]{0:T(1024)(128)(4,1)}), s8[4194304]{0:T(1024)(128)(4,1)S(1)}, s32[]{:S(2)}) async-start(s8[8388608]{0:T(1024)(128)(4,1)} %bitcast.125), calls=%async_computation.7 | async-start | bytes 8388608
  227.5 46.7 %copy-start.3 = (s32[64]{0:T(128)S(1)}, s32[64]{0:T(128)}, u32[]{:S(2)}) copy-start(s32[64]{0:T(128)} %param.15) | copy-start | bytes 772
  227.5 46.8 %copy-start.2 = (f32[2,64]{1,0:T(2,128)S(1)}, f32[2,64]{1,0:T(2,128)}, u32[]{:S(2)}) copy-start(f32[2,64]{1,0:T(2,128)} %param.14) | copy-start | bytes 1540
  227.5 113.4 %copy-start.1 = (f32[2,32,1024]{2,1,0:T(8,128)S(1)}, f32[2,32,1024]{2,1,0:T(8,128)}, u32[]{:S(2)}) copy-start(f32[2,32,1024]{2,1,0:T(8,128)} %param.13) | copy-start | bytes 786436
  227.5 113.3 %reduce-scatter.5.cloned.1.call-start = ((), (), s32[]{:S(2)}) async-start(), calls=%async_computation.5 | async-start | bytes 1310720 | tf_op jit(solution)/shard_map/reduce_scatter | solution.py:36
Sparse Core Ops, SparseCore 0:
  45.7 50.1 all-gather.1
  227.6 46.4 reduce-scatter.2
  276.6 21.9 reduce-scatter.4
